TPU v7x, 32 devices: a whole 2x2x4 slice. The times are simulated.
32 devices in a mesh: groups: 2 (over y), center: 8 (over z, x), row: 2 (over core).
Axes of the slice: x: 2, y: 2, z: 4, core: 2. Of those that a mesh axis runs over, the one named last changes fastest.
Arguments:
- dataset: float32 [512, 1024], P(('groups', 'center', 'row')), parts along dimension 0, may hold values from -0.1875 to 0.1875
- centers: float32 [2048, 1024], P(('groups', 'center')), parts along dimension 0, may hold values from -0.1875 to 0.1875
- weights: float32 [2048, 512], P(('groups', 'center'), 'row'), parts along dimension 0, may hold values from -0.1875 to 0.1875
- batch_index: int32 [2, 128], P(None, ('groups', 'center', 'row')), parts along dimension 1, may hold values from 0 to 15
- targets: float32 [2, 128, 512], P(None, ('groups', 'center', 'row')), parts along dimension 1, may hold values from -6 to 6
- gamma: float32 [2], P('groups'), parts along dimension 0, may hold values from 0.3 to 1.5
Outputs:
- new_weights: float32 [2048, 512], P(('groups', 'center'), 'row'), parts along dimension 0
- residual: float32 [128, 512], P(('groups', 'center', 'row')), parts along dimension 0
There are 2 independent parts, one for each index of `groups`. A program takes and returns all parts, laid end to end along the dimension named above; each array names one. Nothing has to cross between parts.
Inputs may be any that keep to these rules, and one draw needn't show every extreme that they name: `batch_index`: each entry picks a row within the block of 16 dataset rows that has the same block number as the entry's block of 4 batch rows.
All inputs are finite; a program needn't handle non-finite values.
Results may differ from a plain program's by a relative error of at most 0.0001.
Values sent between devices are 32-bit elements; how exact they have to be, the bound alone decides.
A program may use at most 64 MiB of HBM per device.

v0:
```python
import jax
import jax.numpy as jnp
from jax import lax
from jax.sharding import PartitionSpec as P


def per_device(dataset, centers, weights, batch_index, targets, gamma):
    center_sq = jnp.sum(centers * centers, axis=1)
    rows_here = batch_index.shape[1]
    current = weights
    residual = None
    for step in range(2):
        local_rows = dataset[batch_index[step]]
        rows, wanted = (
            lax.all_gather(local_rows, "center", axis=0, tiled=True),
            lax.all_gather(targets[step], "center", axis=0, tiled=True),
        )
        full_weights = lax.all_gather(current, "row", axis=1, tiled=True)
        row_sq = jnp.sum(rows * rows, axis=1)
        cross = jnp.dot(
            rows, centers.T, precision=lax.Precision.HIGHEST, preferred_element_type=jnp.float32
        )
        kernel = jnp.exp(-gamma[0] * (row_sq[:, None] + center_sq[None, :] - 2.0 * cross))
        partial_pred = jnp.dot(
            kernel,
            full_weights,
            precision=lax.Precision.HIGHEST,
            preferred_element_type=jnp.float32,
        )
        summed = lax.psum(partial_pred, "center")
        gathered_res = summed - wanted
        residual = lax.dynamic_slice_in_dim(
            gathered_res, lax.axis_index("center") * rows_here, rows_here, 0
        )
        grad = jnp.dot(
            kernel.T,
            gathered_res,
            precision=lax.Precision.HIGHEST,
            preferred_element_type=jnp.float32,
        )
        own_grad = lax.psum_scatter(grad, "row", scatter_dimension=1, tiled=True)
        batch_total = rows.shape[0] * lax.axis_size("row")
        current = current - 0.5 / batch_total * own_grad
    return (current, residual)


def solution(mesh):
    return jax.shard_map(
        per_device,
        mesh=mesh,
        in_specs=(
            P(("groups", "center", "row"), None),
            P(("groups", "center"), None),
            P(("groups", "center"), "row"),
            P(None, ("groups", "center", "row")),
            P(None, ("groups", "center", "row"), None),
            P("groups"),
        ),
        out_specs=(P(("groups", "center"), "row"), P(("groups", "center", "row"), None)),
        check_vma=False,
    )
```

profile of v0, /device:TPU:0, one launch (start us, length us, event | category | flops | bytes accessed | tf_op | source)
XLA Modules:
  0.0 240.4 jit_solution(545532573906874737)
XLA Ops:
  7.9 1.2 multiply_reduce_fusion
  9.1 0.6 gather_fusion
  9.7 32.3 %all-gather.4 = f32[8,4,1024]{2,1,0:T(4,128)S(1)} all-gather(f32[1,4,1024]{2,1,0:T(4,128)S(1)} %bitcast.27), channel_id=2, replica_groups=mesh['groups'=2,'center'=8,'row'=2] {'center'}, dimensions={0}, use_global_device_ids=true | all-gather | bytes 147456 | tf_op jit(solution)/shard_map/all_gather | solution.py:15
  42.2 0.8 copy-done.2
  42.9 2.0 all_gather.19
  44.9 0.6 fusion.5
  45.5 0.9 fusion.11
  46.5 0.6 copy-done.3
  47.2 30.5 %all-gather.1 = f32[1,32,512]{2,0,1:T(1,128)S(1)} all-gather(f32[1,4,512]{2,0,1:T(1,128)S(1)} %copy.12), channel_id=3, replica_groups=mesh['groups'=2,'center'=8,'row'=2] {'center'}, dimensions={1}, use_global_device_ids=true | all-gather | bytes 73728 | tf_op jit(solution)/shard_map/all_gather | solution.py:16
  77.7 38.4 %all-reduce.3.cloned.1.call-done = f32[32,512]{1,0:T(8,128)} async-done(((f32[32,512]{1,0:T(8,128)}), f32[32,512]{1,0:T(8,128)}) %all-reduce.3.cloned.1.call-update) | async-done | bytes 65552 | tf_op jit(solution)/shard_map/psum | solution.py:30
  116.0 2.0 fusion.6
  118.1 0.6 gather_fusion.1
  118.6 30.5 %all-gather.5 = f32[8,4,1024]{2,1,0:T(4,128)S(1)} all-gather(f32[1,4,1024]{2,1,0:T(4,128)S(1)} %bitcast.28), channel_id=4, replica_groups=mesh['groups'=2,'center'=8,'row'=2] {'center'}, dimensions={0}, use_global_device_ids=true | all-gather | bytes 147456 | tf_op jit(solution)/shard_map/all_gather | solution.py:15
  149.3 0.6 fusion.2
  150.0 0.9 multiply_subtract_fusion.1
  150.9 2.0 all_gather.22
  152.9 0.9 fusion.12
  153.9 30.5 %all-gather.3 = f32[1,32,512]{2,0,1:T(1,128)S(1)} all-gather(f32[1,4,512]{2,0,1:T(1,128)S(1)} %copy.13), channel_id=5, replica_groups=mesh['groups'=2,'center'=8,'row'=2] {'center'}, dimensions={1}, use_global_device_ids=true | all-gather | bytes 73728 | tf_op jit(solution)/shard_map/all_gather | solution.py:16
  184.4 38.1 %all-reduce.5.cloned.1.call-done = f32[32,512]{1,0:T(8,128)} async-done(((f32[32,512]{1,0:T(8,128)}), f32[32,512]{1,0:T(8,128)}) %all-reduce.5.cloned.1.call-update) | async-done | bytes 65552 | tf_op jit(solution)/shard_map/psum | solution.py:30
  222.5 0.8 bitcast_subtract_fusion
  223.3 1.1 fusion.13
  224.5 0.6 constant_dynamic-slice_fusion
  225.1 7.2 %reduce-scatter.5.cloned.1.call-done = f32[128,256]{1,0:T(8,128)} async-done(((f32[128,512]{1,0:T(8,128)}), f32[128,256]{1,0:T(8,128)}) %reduce-scatter.5.cloned.1.call-update) | async-done | bytes 131088 | tf_op jit(solution)/shard_map/reduce_scatter | solution.py:41
  232.3 1.6 multiply_subtract_fusion
  (26 shorter events, 0.6 us)
Async XLA Ops:
  7.2 1.9 copy-start
  7.2 108.9 %all-reduce.3.cloned.1.call-start = ((), (), s32[]{:S(2)}) async-start(), calls=%async_computation.2 | async-start | bytes 131072 | tf_op jit(solution)/shard_map/psum | solution.py:30
  7.9 1.2 copy-start.4
  9.1 35.8 %copy-start.1 = (f32[128,1024]{1,0:T(8,128)S(1)}, f32[128,1024]{1,0:T(8,128)}, u32[]{:S(2)}) copy-start(f32[128,1024]{1,0:T(8,128)} %param.7) | copy-start | bytes 1572868
  42.0 0.9 copy-start.2
  46.4 0.7 copy-start.3
  46.5 103.5 %reduce-scatter.3.cloned.1.call-start = ((), (), s32[]{:S(2)}) async-start(), calls=%async_computation.3 | async-start | bytes 393216 | tf_op jit(solution)/shard_map/reduce_scatter | solution.py:41
  118.0 104.5 %all-reduce.5.cloned.1.call-start = ((), (), s32[]{:S(2)}) async-start(), calls=%async_computation.4 | async-start | bytes 131072 | tf_op jit(solution)/shard_map/psum | solution.py:30
  153.8 78.5 %reduce-scatter.5.cloned.1.call-start = ((), (), s32[]{:S(2)}) async-start(), calls=%async_computation.5 | async-start | bytes 393216 | tf_op jit(solution)/shard_map/reduce_scatter | solution.py:41
Sparse Core Ops, SparseCore 0:
  46.6 69.4 all-reduce.2
  118.3 7.5 reduce-scatter.2
  153.9 68.4 all-reduce.4
  224.6 7.5 reduce-scatter.4
where the time goes:
time: 241 us; the launch traced here: 240 us
  blocking collectives  128 us (53%)
  waiting for transfers between devices  83.7 us (35%)
  between operations  14.5 us (6%)
  matrix products  6.1 us (3%)
  other arithmetic  4.76 us (2%)
  local copies, waits for them, and re-layouts  3.3 us (1%)
    psum x2, waiting for transfers between devices, per_device(): summed = lax.psum(partial_pred, 'center')  76.4 us
    all_gather x2, blocking collectives, per_device(): lax.all_gather(local_rows, 'center', axis=0, tiled=True)  62.8 us
    all_gather x2, blocking collectives, per_device(): lax.all_gather(targets[step], 'center', axis=0, tiled=True)  61 us
    reduce_scatter x2, waiting for transfers between devices, per_device(): own_grad = lax.psum_scatter(grad, 'row', scatter_dimension=1, tiled=True)  7.22 us
  transfers between devices with their start and end apart: 4, of which 3 were waited for; matrix products, arithmetic and copies ran while one was open for 1% of the time, Pallas kernels for 0%

commit v1 on v0

v1 whole, which is shorter than its diff:
```python
import functools

import jax
import jax.numpy as jnp
from jax import lax
from jax.experimental import pallas as pl
from jax.experimental.pallas import tpu as pltpu
from jax.sharding import PartitionSpec as P

MESH = pl.DeviceIdType.MESH
LANES = 128
NN = (((1,), (0,)), ((), ()))
NT = (((1,), (1,)), ((), ()))
UNROLL = 8


def split(v):
    hi = v.astype(jnp.bfloat16)
    return hi, (v - hi.astype(jnp.float32)).astype(jnp.bfloat16)


def dot3(a, b, dims=NN):
    (ah, al), (bh, bl) = a, b
    dot = functools.partial(lax.dot_general, dimension_numbers=dims, preferred_element_type=jnp.float32)
    return dot(ah, bh) + (dot(ah, bl) + dot(al, bh))


def each(lo, hi, body):
    if hi - lo <= UNROLL:
        for d in range(lo, hi):
            body(d)
    else:
        lax.fori_loop(lo, hi, lambda d, _: (body(d), 0)[1], 0)


def kernel(
    n, ds_ref, cen_ref, w_ref, idx_ref, tgt_ref, gam_ref, w_out, res_out,
    xbuf, kbuf, tsib, tplace, part, rs_in, allv, res_s, rsend, rrecv,
    x_ss, x_rs, p_ss, p_rs, a_ss, a_rs, s_ss, s_rs,
):
    f32 = jnp.float32
    c, r = lax.axis_index("center"), lax.axis_index("row")
    sib = 1 - r
    steps, rows = idx_ref.shape
    slot = steps * rows
    chunks = 2 * n
    total = slot * chunks
    batch = rows * chunks
    cols = w_ref.shape[1]
    ncen = cen_ref.shape[0]
    rate = 0.5 / batch
    rp, rg = total // n, batch // n
    pw, gw = cols // LANES, pl.cdiv(batch, LANES)

    barrier = pltpu.get_barrier_semaphore()

    def greet(d):
        pl.semaphore_signal(
            barrier, inc=1, device_id={"center": lax.rem(c + d, n), "row": r}, device_id_type=MESH
        )

    each(1, n, greet)
    pl.semaphore_signal(barrier, inc=1, device_id={"center": c, "row": sib}, device_id_type=MESH)

    def copy(src, dst, ss, rs, peer):
        return pltpu.make_async_remote_copy(
            src_ref=src, dst_ref=dst, send_sem=ss, recv_sem=rs, device_id=peer, device_id_type=MESH
        )

    def to(d):
        return {"center": lax.rem(c + d, n), "row": r}

    to_sib = {"center": c, "row": sib}

    for b in range(steps):
        for i in range(rows):
            xbuf[c, pl.ds(b * rows + i, 1), :] = ds_ref[pl.ds(idx_ref[b, i], 1), :]

    pl.semaphore_wait(barrier, n)

    def x_copy(d):
        return copy(xbuf.at[c], xbuf.at[c], x_ss.at[d], x_rs.at[d], to(d))

    each(1, n, lambda d: x_copy(d).start())
    sib_cols = pl.ds(pl.multiple_of(sib * cols, LANES), cols)
    own_cols = pl.ds(pl.multiple_of(r * cols, LANES), cols)
    t_copy = copy(tgt_ref.at[:, :, sib_cols], tsib, s_ss.at[0], s_rs.at[0], to_sib)
    t_copy.start()

    cen = cen_ref[...]
    cen2 = split(cen)
    csq = jnp.sum(cen * cen, axis=1, keepdims=True)
    csq = jnp.transpose(jnp.broadcast_to(csq, (ncen, ncen)))[0:1, :]
    w2 = split(w_ref[...])
    gamma = gam_ref[0]

    t_copy.wait()
    chunk_id = lax.broadcasted_iota(jnp.int32, (chunks, cols), 0)
    for b in range(steps):
        mine, other = tgt_ref[b, :, own_cols], tsib[b]
        for i in range(rows):
            j = b * rows + i
            placed = jnp.where(chunk_id == r * n + c, mine[i : i + 1, :], 0.0)
            placed = jnp.where(chunk_id == sib * n + c, other[i : i + 1, :], placed)
            tplace[pl.ds(j * chunks, chunks), :] = placed

    each(1, n, lambda d: x_copy(d).wait_recv())

    blocks = max(1, n // UNROLL)
    per = n // blocks
    k_base = pl.multiple_of(r * (n * slot), slot)

    def kernel_rows(s):
        x = xbuf[pl.ds(s * per, per)].reshape(per * slot, xbuf.shape[2])
        xsq = jnp.sum(x * x, axis=1, keepdims=True)
        cross = dot3(split(x), cen2, NT)
        kbuf[pl.ds(pl.multiple_of(k_base + s * (per * slot), slot), per * slot), :] = jnp.exp(
            -gamma * (xsq + csq - 2.0 * cross)
        )

    each(0, blocks, kernel_rows)
    k_rows = pl.ds(k_base, n * slot)
    k_copy = copy(kbuf.at[k_rows, :], kbuf.at[k_rows, :], s_ss.at[1], s_rs.at[1], to_sib)
    k_copy.start()
    k_copy.wait()

    k_all = jnp.concatenate([kbuf[pl.ds(j, chunks, stride=slot), :] for j in range(slot)], axis=0)
    kh, kl = split(k_all)
    k0 = (kh[: gw * LANES], kl[: gw * LANES])
    k_t = split(jnp.transpose(k_all))

    for s in range(blocks):
        own = pl.ds(s * per, per)
        lo, hi = s * per * rp, (s + 1) * per * rp
        p = dot3((kh[lo:hi], kl[lo:hi]), w2) - tplace[lo:hi, :]
        lo, hi = batch + s * per * rg, batch + (s + 1) * per * rg
        g = dot3((kh[lo:hi], kl[lo:hi]), k0, NT)
        for l in range(pw):
            part[own, l * rp : (l + 1) * rp, :] = p[:, l * LANES : (l + 1) * LANES].reshape(per, rp, LANES)
        for l in range(gw):
            at = pw * rp + l * rg
            part[own, at : at + rg, :] = g[:, l * LANES : (l + 1) * LANES].reshape(per, rg, LANES)

    def p_copy(d):
        return copy(part.at[lax.rem(c + d, n)], rs_in.at[d], p_ss.at[d], p_rs.at[d], to(d))

    each(1, n, lambda d: p_copy(d).start())
    allv[c] = part[c]

    def add(d):
        p_copy(d).wait_recv()
        allv[c] += rs_in[d]

    each(1, n, add)

    def a_copy(d):
        return copy(allv.at[c], allv.at[c], a_ss.at[d], a_rs.at[d], to(d))

    each(1, n, lambda d: a_copy(d).start())
    each(1, n, lambda d: a_copy(d).wait_recv())

    def whole(at, size, width):
        pieces = [
            allv[:, at + l * size : at + (l + 1) * size, :].reshape(n * size, LANES) for l in range(width)
        ]
        return pieces[0] if width == 1 else jnp.concatenate(pieces, axis=1)

    a = whole(0, rp, pw)
    g = whole(pw * rp, rg, gw)
    res0 = a[:batch]
    pad = gw * LANES - batch
    res0_pad = jnp.concatenate([res0, jnp.zeros((pad, cols), f32)], axis=0) if pad else res0
    res1 = a[batch:] - rate * dot3(split(g), split(res0_pad))
    res_s[...] = res1
    for i in range(rows):
        rsend[i : i + 1, :] = res_s[pl.ds(i * chunks + sib * n + c, 1), :]
    r_copy = copy(rsend, rrecv, s_ss.at[2], s_rs.at[2], to_sib)
    r_copy.start()
    for i in range(rows):
        res_out[i : i + 1, own_cols] = res_s[pl.ds(i * chunks + r * n + c, 1), :]
    res = jnp.concatenate([res0, res1], axis=0)
    w_out[...] = w_ref[...] - rate * dot3(k_t, split(res))
    r_copy.wait()
    res_out[:, sib_cols] = rrecv[...]

    def drain(d):
        x_copy(d).wait_send()
        p_copy(d).wait_send()
        a_copy(d).wait_send()

    each(1, n, drain)


def solution(mesh):
    n = mesh.shape["center"]

    def per_device(dataset, centers, weights, batch_index, targets, gamma):
        f32 = jnp.float32
        steps, rows = batch_index.shape
        slot, feats = steps * rows, dataset.shape[1]
        ncen, cols = weights.shape
        total, batch = slot * 2 * n, rows * 2 * n
        rp, rg = total // n, batch // n
        pw, gw = cols // LANES, pl.cdiv(batch, LANES)
        height = pw * rp + gw * rg
        vm = pltpu.VMEM
        dma = pltpu.SemaphoreType.DMA
        return pl.pallas_call(
            functools.partial(kernel, n),
            out_shape=(
                jax.ShapeDtypeStruct(weights.shape, f32),
                jax.ShapeDtypeStruct(targets.shape[1:], f32),
            ),
            in_specs=[
                pl.BlockSpec(memory_space=pltpu.VMEM),
                pl.BlockSpec(memory_space=pltpu.VMEM),
                pl.BlockSpec(memory_space=pltpu.VMEM),
                pl.BlockSpec(memory_space=pltpu.SMEM),
                pl.BlockSpec(memory_space=pltpu.VMEM),
                pl.BlockSpec(memory_space=pltpu.SMEM),
            ],
            out_specs=(pl.BlockSpec(memory_space=pltpu.VMEM), pl.BlockSpec(memory_space=pltpu.VMEM)),
            scratch_shapes=[
                vm((n, slot, feats), f32),
                vm((2 * n * slot, ncen), f32),
                vm((steps, rows, cols), f32),
                vm((total, cols), f32),
                vm((n, height, LANES), f32),
                vm((n, height, LANES), f32),
                vm((n, height, LANES), f32),
                vm((batch, cols), f32),
                vm((rows, cols), f32),
                vm((rows, cols), f32),
                dma((n,)), dma((n,)), dma((n,)), dma((n,)), dma((n,)), dma((n,)), dma((3,)), dma((3,)),
            ],
            compiler_params=pltpu.CompilerParams(
                collective_id=0, has_side_effects=True, vmem_limit_bytes=56 * 2**20
            ),
        )(dataset, centers, weights, batch_index, targets, gamma)

    return jax.shard_map(
        per_device,
        mesh=mesh,
        in_specs=(
            P(("groups", "center", "row"), None),
            P(("groups", "center"), None),
            P(("groups", "center"), "row"),
            P(None, ("groups", "center", "row")),
            P(None, ("groups", "center", "row"), None),
            P("groups"),
        ),
        out_specs=(P(("groups", "center"), "row"), P(("groups", "center", "row"), None)),
        check_vma=False,
    )
```

time: 241 us -> 31.8 us (0.13)
  blocking collectives: 128 us -> 0 us
  waiting for transfers between devices: 83.7 us -> 0 us
  Pallas kernels: 0 us -> 28.1 us
  between operations: 14.5 us -> 1.29 us
  matrix products: 6.1 us -> 0 us
  other arithmetic: 4.76 us -> 0 us
    all_gather x6 -> x0, blocking collectives: 128 us -> none  [the longest x2 62.8 us: per_device(): lax.all_gather(local_rows, 'center', axis=0, tiled=True)]
    psum x2 -> x0, waiting for transfers between devices: 76.4 us -> none  [per_device(): summed = lax.psum(partial_pred, 'center')]
    pallas_call x0 -> x1, Pallas kernels: none -> 28.1 us  [per_device(): pl.pallas_call(functools.partial(kernel, n), out_shape=(jax.ShapeDtypeStr...]
    reduce_scatter x2 -> x0, waiting for transfers between devices: 7.22 us -> none  [per_device(): own_grad = lax.psum_scatter(grad, 'row', scatter_dimension=1, tiled=True)]
    dot_general x6 -> x0, matrix products: 6.1 us -> none  [the longest x2 3.07 us: per_device(): jnp.dot(kernel.T, gathered_res, precision=lax.Precision.HIGHEST, preferre...]
    sub x3 -> x0, other arithmetic: 3.35 us -> none  [the longest x2 2.5 us: per_device(): current = current - 0.5 / batch_total * own_grad]
  transfers between devices with their start and end apart: 4 -> 0, of which waited for: 3 -> 0; matrix products, arithmetic and copies ran while one was open for 1% -> 0% of each run, Pallas kernels for 0% -> 0%
where the time goes in v1:
time: 31.8 us; the launch traced here: 31.6 us
  Pallas kernels  28.1 us (88%)
  local copies, waits for them, and re-layouts  2.18 us (7%)
  between operations  1.29 us (4%)
    pallas_call x1, Pallas kernels, per_device(): pl.pallas_call(functools.partial(kernel, n), out_shape=(jax.ShapeDtypeStr...  28.1 us
    unnamed x4, local copies, waits for them, and re-layouts  2.18 us

profile of v1, /device:TPU:0, one launch (start us, length us, event | category | flops | bytes accessed | tf_op | source)
XLA Modules:
  0.0 31.6 jit_solution(1502628400446209146)
XLA Ops:
  1.3 28.1 %shard_map.77 = (f32[128,256]{1,0:T(8,128)}, f32[4,512]{1,0:T(4,128)}) custom-call(f32[16,1024]{1,0:T(8,128)} %ds_ref.1, f32[128,1024]{1,0:T(8,128)} %cen_ref.1, f32[128,256]{1,0:T(8,128)} %w_ref.1, s32[2,4]{1,0:T(2,128)} %idx_ref.1, f32[2,4,512]{2,1,0:T(4,128)} %tgt_ref.1, f32[1]{0:T(128)S(6)} %copy.10.gam_ref), custom_call_target="tpu_custom_call" | custom-call | tf_op jit(solution)/shard_map/pallas_call | solution.py:208
  29.4 0.0 copy-start
  29.4 1.6 %copy.11 = f32[128,256]{1,0:T(8,128)} copy(f32[128,256]{1,0:T(8,128)} %get-tuple-element.4) | data formatting | bytes 262144
  31.0 0.0 copy-done
  31.0 0.6 %copy.12 = f32[4,512]{1,0:T(4,128)} copy(f32[4,512]{1,0:T(4,128)S(1)} %copy-done) | data formatting | bytes 16384
Async XLA Ops:
  29.4 1.6 %copy-start = (f32[4,512]{1,0:T(4,128)S(1)}, f32[4,512]{1,0:T(4,128)}, u32[]{:S(2)}) copy-start(f32[4,512]{1,0:T(4,128)} %get-tuple-element.5) | copy-start | bytes 24580

commit v2 on v1

v2 whole, which is shorter than its diff:
```python
import functools

import jax
import jax.numpy as jnp
from jax import lax
from jax.experimental import pallas as pl
from jax.experimental.pallas import tpu as pltpu
from jax.sharding import PartitionSpec as P

MESH = pl.DeviceIdType.MESH
LANES = 128
NN = (((1,), (0,)), ((), ()))
NT = (((1,), (1,)), ((), ()))
UNROLL = 8


def split(v):
    hi = v.astype(jnp.bfloat16)
    return hi, (v - hi.astype(jnp.float32)).astype(jnp.bfloat16)


def dot3(a, b, dims=NN):
    (ah, al), (bh, bl) = a, b
    dot = functools.partial(lax.dot_general, dimension_numbers=dims, preferred_element_type=jnp.float32)
    return dot(ah, bh) + (dot(ah, bl) + dot(al, bh))


def each(lo, hi, body):
    if hi - lo <= UNROLL:
        for d in range(lo, hi):
            body(d)
    else:
        lax.fori_loop(lo, hi, lambda d, _: (body(d), 0)[1], 0)


def kernel(
    n, ds_hbm, cen_hbm, w_hbm, idx_hbm, tgt_hbm, gam_hbm, w_out, res_out,
    ds_ref, cen_ref, w_ref, idx_ref, tgt_ref, gam_ref,
    xbuf, kbuf, tsib, tplace, part, rs_in, allv, res_s, rsend, rrecv,
    in_s, x_ss, x_rs, f_ss, f_rs, p_ss, p_rs, a_ss, a_rs, s_ss, s_rs,
):
    f32 = jnp.float32
    c, r = lax.axis_index("center"), lax.axis_index("row")
    sib = 1 - r
    half = n // 2
    h, side = c // 2, lax.rem(c, 2)
    place = side * half + h
    steps, rows = idx_ref.shape
    slot = steps * rows
    chunks = 2 * n
    batch = rows * chunks
    cols = w_ref.shape[1]
    ncen = cen_ref.shape[0]
    rate = 0.5 / batch
    fold, rp, rg, pw, gw = sizes(n, batch, steps, cols)

    ins = [
        pltpu.make_async_copy(src, dst, in_s.at[i])
        for i, (src, dst) in enumerate(
            [(idx_hbm, idx_ref), (ds_hbm, ds_ref), (tgt_hbm, tgt_ref), (cen_hbm, cen_ref), (w_hbm, w_ref), (gam_hbm, gam_ref)]
        )
    ]
    for one in ins:
        one.start()

    barrier = pltpu.get_barrier_semaphore()

    def to(d):
        return {"center": lax.rem(c + d, n), "row": r}

    to_sib = {"center": c, "row": sib}
    to_pair = {"center": 2 * h + 1 - side, "row": r}
    each(1, n, lambda d: pl.semaphore_signal(barrier, inc=1, device_id=to(d), device_id_type=MESH))
    pl.semaphore_signal(barrier, inc=1, device_id=to_sib, device_id_type=MESH)

    def copy(src, dst, ss, rs, peer):
        return pltpu.make_async_remote_copy(
            src_ref=src, dst_ref=dst, send_sem=ss, recv_sem=rs, device_id=peer, device_id_type=MESH
        )

    ins[0].wait()
    ins[1].wait()
    for b in range(steps):
        for i in range(rows):
            xbuf[place, pl.ds(b * rows + i, 1), :] = ds_ref[pl.ds(idx_ref[b, i], 1), :]
    ins[2].wait()

    pl.semaphore_wait(barrier, n)

    def x_copy(e):
        peer = {"center": 2 * lax.rem(h + e, half) + side, "row": r}
        return copy(xbuf.at[place], xbuf.at[place], x_ss.at[e], x_rs.at[e], peer)

    def f_copy(e):
        at = side * half + lax.rem(h + half - e, half)
        return copy(xbuf.at[at], xbuf.at[at], f_ss.at[e], f_rs.at[e], to_pair)

    each(1, half, lambda e: x_copy(e).start())
    f_copy(0).start()
    sib_cols = pl.ds(pl.multiple_of(sib * cols, LANES), cols)
    own_cols = pl.ds(pl.multiple_of(r * cols, LANES), cols)
    t_copy = copy(tgt_ref.at[:, :, sib_cols], tsib, s_ss.at[0], s_rs.at[0], to_sib)
    t_copy.start()

    ins[3].wait()
    cen = cen_ref[...]
    cen2 = split(cen)
    csq = jnp.sum(cen * cen, axis=1, keepdims=True)
    csq = jnp.transpose(jnp.broadcast_to(csq, (ncen, ncen)))[0:1, :]
    ins[4].wait()
    w2 = split(w_ref[...])
    ins[5].wait()
    gamma = gam_ref[0]

    def pass_on(e):
        x_copy(e).wait_recv()
        f_copy(e).start()

    each(1, half, pass_on)

    count = half * slot
    step = min(count, UNROLL * slot)

    def kernel_rows(which, s):
        first = pl.multiple_of(which * count + s * step, slot)
        x = xbuf[pl.ds(which * half + s * (step // slot), step // slot)].reshape(step, xbuf.shape[2])
        xsq = jnp.sum(x * x, axis=1, keepdims=True)
        cross = dot3(split(x), cen2, NT)
        kbuf[pl.ds(pl.multiple_of(r * (n * slot) + first, slot), step), :] = jnp.exp(
            -gamma * (xsq + csq - 2.0 * cross)
        )

    def k_copy(i, which):
        at = pl.ds(pl.multiple_of(r * (n * slot) + which * count, slot), count)
        return copy(kbuf.at[at, :], kbuf.at[at, :], s_ss.at[i], s_rs.at[i], to_sib)

    each(0, count // step, lambda s: kernel_rows(side, s))
    k_copy(1, side).start()

    t_copy.wait()
    chunk_id = lax.broadcasted_iota(jnp.int32, (chunks, cols), 0)
    for b in range(steps):
        mine, other = tgt_ref[b, :, own_cols], tsib[b]
        for i in range(rows):
            j = b * rows + i
            placed = jnp.where(chunk_id == r * n + place, mine[i : i + 1, :], 0.0)
            placed = jnp.where(chunk_id == sib * n + place, other[i : i + 1, :], placed)
            tplace[pl.ds(j * chunks, chunks), :] = placed

    each(0, half, lambda e: f_copy(e).wait_recv())
    each(0, count // step, lambda s: kernel_rows(1 - side, s))
    k_copy(2, 1 - side).start()
    k_copy(1, side).wait()
    k_copy(2, 1 - side).wait()

    k_all = jnp.concatenate([kbuf[pl.ds(j, chunks, stride=slot), :] for j in range(slot)], axis=0)
    kh, kl = split(k_all)
    k0 = (jnp.concatenate([kh[:batch]] * fold, axis=0), jnp.concatenate([kl[:batch]] * fold, axis=0))

    blocks = max(1, n // UNROLL)
    per = n // blocks
    for s in range(blocks):
        lo, hi = s * per * rp, (s + 1) * per * rp
        p = dot3((kh[lo:hi], kl[lo:hi]), w2) - tplace[lo:hi, :]
        lo, hi = batch + s * per * rg * fold, batch + (s + 1) * per * rg * fold
        g = fold_rows(dot3((kh[lo:hi], kl[lo:hi]), k0, NT), fold, batch)
        for o in range(per):
            for l in range(pw):
                part[s * per + o, l * rp : (l + 1) * rp, :] = p[o * rp : (o + 1) * rp, l * LANES : (l + 1) * LANES]
            for l in range(gw):
                at = pw * rp + l * rg
                part[s * per + o, at : at + rg, :] = g[o * rg : (o + 1) * rg, l * LANES : (l + 1) * LANES]

    def p_copy(d):
        return copy(part.at[lax.rem(c + d, n)], rs_in.at[d], p_ss.at[d], p_rs.at[d], to(d))

    each(1, n, lambda d: p_copy(d).start())
    k_t = split(jnp.transpose(k_all))
    allv[c] = part[c]

    def add(d):
        p_copy(d).wait_recv()
        allv[c] += rs_in[d]

    each(1, n, add)

    def a_copy(d):
        return copy(allv.at[c], allv.at[c], a_ss.at[d], a_rs.at[d], to(d))

    each(1, n, lambda d: a_copy(d).start())
    each(1, n, lambda d: a_copy(d).wait_recv())

    def whole(at, size, width):
        pieces = [
            jnp.concatenate([allv[o, at + l * size : at + (l + 1) * size, :] for o in range(n)], axis=0)
            for l in range(width)
        ]
        return pieces[0] if width == 1 else jnp.concatenate(pieces, axis=1)

    a = whole(0, rp, pw)
    g = unfold_rows(whole(pw * rp, rg, gw), fold, batch)
    res0 = a[:batch]
    res0h, res0l = split(res0)
    res0f = (jnp.concatenate([res0h] * fold, axis=0), jnp.concatenate([res0l] * fold, axis=0))
    res1 = a[batch:] - rate * dot3(split(g), res0f)
    res_s[...] = res1
    for i in range(rows):
        rsend[i : i + 1, :] = res_s[pl.ds(i * chunks + sib * n + place, 1), :]
    r_copy = copy(rsend, rrecv, s_ss.at[3], s_rs.at[3], to_sib)
    r_copy.start()
    for i in range(rows):
        res_out[i : i + 1, own_cols] = res_s[pl.ds(i * chunks + r * n + place, 1), :]
    res1h, res1l = split(res1)
    res = (jnp.concatenate([res0h, res1h], axis=0), jnp.concatenate([res0l, res1l], axis=0))
    w_out[...] = w_ref[...] - rate * dot3(k_t, res)
    r_copy.wait()
    res_out[:, sib_cols] = rrecv[...]

    def drain(d):
        p_copy(d).wait_send()
        a_copy(d).wait_send()

    each(1, n, drain)
    each(1, half, lambda e: x_copy(e).wait_send())
    each(0, half, lambda e: f_copy(e).wait_send())


def sizes(n, batch, steps, cols):
    fold = max(1, LANES // batch)
    return fold, steps * batch // n, batch // fold // n, cols // LANES, pl.cdiv(batch, LANES)


def fold_rows(g, fold, batch):
    if fold == 1:
        return g
    height = g.shape[0] // fold
    at = lax.broadcasted_iota(jnp.int32, (height, LANES), 1) // batch
    out = g[:height]
    for f in range(1, fold):
        out = jnp.where(at == f, g[f * height : (f + 1) * height], out)
    return out


def unfold_rows(g, fold, batch):
    if fold == 1:
        return g
    at = lax.broadcasted_iota(jnp.int32, g.shape, 1) // batch
    return jnp.concatenate([jnp.where(at == f, g, 0.0) for f in range(fold)], axis=0)


def hand_over(w_in, res_in, w_out, res_out, sems):
    copies = [
        pltpu.make_async_copy(w_in, w_out, sems.at[0]),
        pltpu.make_async_copy(res_in, res_out, sems.at[1]),
    ]
    for one in copies:
        one.start()
    for one in copies:
        one.wait()


def solution(mesh):
    n = mesh.shape["center"]

    def per_device(dataset, centers, weights, batch_index, targets, gamma):
        f32 = jnp.float32
        steps, rows = batch_index.shape
        slot, feats = steps * rows, dataset.shape[1]
        ncen, cols = weights.shape
        total, batch = slot * 2 * n, rows * 2 * n
        fold, rp, rg, pw, gw = sizes(n, batch, steps, cols)
        height = pw * rp + gw * rg
        half = n // 2
        vm = pltpu.VMEM
        dma = pltpu.SemaphoreType.DMA
        anywhere = pl.BlockSpec(memory_space=pltpu.HBM)
        outs = (
            jax.ShapeDtypeStruct(weights.shape, f32),
            jax.ShapeDtypeStruct(targets.shape[1:], f32),
        )
        results = pl.pallas_call(
            functools.partial(kernel, n),
            out_shape=outs,
            in_specs=[anywhere] * 6,
            out_specs=(pl.BlockSpec(memory_space=pltpu.VMEM), pl.BlockSpec(memory_space=pltpu.VMEM)),
            scratch_shapes=[
                vm(dataset.shape, f32), vm(centers.shape, f32), vm(weights.shape, f32),
                pltpu.SMEM(batch_index.shape, jnp.int32), vm(targets.shape, f32), pltpu.SMEM(gamma.shape, f32),
                vm((n, slot, feats), f32),
                vm((2 * n * slot, ncen), f32),
                vm((steps, rows, cols), f32),
                vm((total, cols), f32),
                vm((n, height, LANES), f32),
                vm((n, height, LANES), f32),
                vm((n, height, LANES), f32),
                vm((batch, cols), f32),
                vm((rows, cols), f32),
                vm((rows, cols), f32),
                dma((6,)), dma((half,)), dma((half,)), dma((half,)), dma((half,)),
                dma((n,)), dma((n,)), dma((n,)), dma((n,)), dma((4,)), dma((4,)),
            ],
            compiler_params=pltpu.CompilerParams(
                collective_id=0, has_side_effects=True, vmem_limit_bytes=56 * 2**20
            ),
        )(dataset, centers, weights, batch_index, targets, gamma)
        return pl.pallas_call(
            hand_over,
            out_shape=outs,
            in_specs=[anywhere] * 2,
            out_specs=(anywhere, anywhere),
            scratch_shapes=[dma((2,))],
            compiler_params=pltpu.CompilerParams(vmem_limit_bytes=60 * 2**20),
        )(*results)

    return jax.shard_map(
        per_device,
        mesh=mesh,
        in_specs=(
            P(("groups", "center", "row"), None),
            P(("groups", "center"), None),
            P(("groups", "center"), "row"),
            P(None, ("groups", "center", "row")),
            P(None, ("groups", "center", "row"), None),
            P("groups"),
        ),
        out_specs=(P(("groups", "center"), "row"), P(("groups", "center", "row"), None)),
        check_vma=False,
    )
```

time: 31.8 us -> 34.1 us (1.072)
  Pallas kernels: 28.1 us -> 32.6 us
  local copies, waits for them, and re-layouts: 2.18 us -> 0 us
    pallas_call x1 -> x2, Pallas kernels: 28.1 us -> 32.6 us  [the longest x1 27.3 us: per_device(): pl.pallas_call(functools.partial(kernel, n), out_shape=outs, in_specs=[an...]
    unnamed x4 -> x0, local copies, waits for them, and re-layouts: 2.18 us -> none
where the time goes in v2:
time: 34.1 us; the launch traced here: 33.9 us
  Pallas kernels  32.6 us (96%)
  between operations  1.29 us (4%)
    pallas_call x1, Pallas kernels, per_device(): pl.pallas_call(functools.partial(kernel, n), out_shape=outs, in_specs=[an...  27.3 us
    pallas_call x1, Pallas kernels, per_device(): pl.pallas_call(hand_over, out_shape=outs, in_specs=[anywhere] * 2, out_sp...  5.34 us

profile of v2, /device:TPU:0, one launch (start us, length us, event | category | flops | bytes accessed | tf_op | source)
XLA Modules:
  0.0 33.9 jit_solution(6079871891251293166)
XLA Ops:
  1.3 27.3 %shard_map.77 = (f32[128,256]{1,0:T(8,128)}, f32[4,512]{1,0:T(4,128)}) custom-call(f32[16,1024]{1,0:T(8,128)} %ds_hbm.1, f32[128,1024]{1,0:T(8,128)} %cen_hbm.1, f32[128,256]{1,0:T(8,128)} %w_hbm.1, s32[2,4]{1,0:T(2,128)} %idx_hbm.1, f32[2,4,512]{2,1,0:T(4,128)} %tgt_hbm.1, f32[1]{0:T(128)S(6)} %copy.8.gam_hbm), custom_call_target="tpu_custom_call" | custom-call | tf_op jit(solution)/shard_map/pallas_call | solution.py:281
  28.6 5.3 %shard_map.78 = (f32[128,256]{1,0:T(8,128)}, f32[4,512]{1,0:T(4,128)}) custom-call(f32[128,256]{1,0:T(8,128)} %get-tuple-element.4.w_in, f32[4,512]{1,0:T(4,128)} %get-tuple-element.5.res_in), custom_call_target="tpu_custom_call" | custom-call | tf_op jit(solution)/shard_map/pallas_call | solution.py:306

commit v3 on v2

--- a/solution.py
+++ b/solution.py
@@ -34,8 +34,8 @@
 
 
 def kernel(
-    n, ds_hbm, cen_hbm, w_hbm, idx_hbm, tgt_hbm, gam_hbm, w_out, res_out,
-    ds_ref, cen_ref, w_ref, idx_ref, tgt_ref, gam_ref,
+    n, ds_hbm, cen_hbm, w_hbm, idx_hbm, tgt_hbm, gam_ref, w_out, res_out,
+    ds_ref, cen_ref, w_ref, idx_ref, tgt_ref,
     xbuf, kbuf, tsib, tplace, part, rs_in, allv, res_s, rsend, rrecv,
     in_s, x_ss, x_rs, f_ss, f_rs, p_ss, p_rs, a_ss, a_rs, s_ss, s_rs,
 ):
@@ -57,7 +57,7 @@
     ins = [
         pltpu.make_async_copy(src, dst, in_s.at[i])
         for i, (src, dst) in enumerate(
-            [(idx_hbm, idx_ref), (ds_hbm, ds_ref), (tgt_hbm, tgt_ref), (cen_hbm, cen_ref), (w_hbm, w_ref), (gam_hbm, gam_ref)]
+            [(idx_hbm, idx_ref), (ds_hbm, ds_ref), (tgt_hbm, tgt_ref), (cen_hbm, cen_ref), (w_hbm, w_ref)]
         )
     ]
     for one in ins:
@@ -109,7 +109,6 @@
     csq = jnp.transpose(jnp.broadcast_to(csq, (ncen, ncen)))[0:1, :]
     ins[4].wait()
     w2 = split(w_ref[...])
-    ins[5].wait()
     gamma = gam_ref[0]
 
     def pass_on(e):
@@ -281,11 +280,11 @@
         results = pl.pallas_call(
             functools.partial(kernel, n),
             out_shape=outs,
-            in_specs=[anywhere] * 6,
+            in_specs=[anywhere] * 5 + [pl.BlockSpec(memory_space=pltpu.SMEM)],
             out_specs=(pl.BlockSpec(memory_space=pltpu.VMEM), pl.BlockSpec(memory_space=pltpu.VMEM)),
             scratch_shapes=[
                 vm(dataset.shape, f32), vm(centers.shape, f32), vm(weights.shape, f32),
-                pltpu.SMEM(batch_index.shape, jnp.int32), vm(targets.shape, f32), pltpu.SMEM(gamma.shape, f32),
+                pltpu.SMEM(batch_index.shape, jnp.int32), vm(targets.shape, f32),
                 vm((n, slot, feats), f32),
                 vm((2 * n * slot, ncen), f32),
                 vm((steps, rows, cols), f32),
@@ -296,20 +295,23 @@
                 vm((batch, cols), f32),
                 vm((rows, cols), f32),
                 vm((rows, cols), f32),
-                dma((6,)), dma((half,)), dma((half,)), dma((half,)), dma((half,)),
+                dma((5,)), dma((half,)), dma((half,)), dma((half,)), dma((half,)),
                 dma((n,)), dma((n,)), dma((n,)), dma((n,)), dma((4,)), dma((4,)),
             ],
             compiler_params=pltpu.CompilerParams(
-                collective_id=0, has_side_effects=True, vmem_limit_bytes=56 * 2**20
+                collective_id=0, has_side_effects=True, vmem_limit_bytes=min(56, 8 + 3 * n) * 2**20
             ),
-        )(dataset, centers, weights, batch_index, targets, gamma)
+        )(*[
+            pltpu.with_memory_space_constraint(v, pltpu.HBM)
+            for v in (dataset, centers, weights, batch_index, targets)
+        ], gamma)
         return pl.pallas_call(
             hand_over,
             out_shape=outs,
-            in_specs=[anywhere] * 2,
+            in_specs=[pl.BlockSpec(memory_space=pltpu.VMEM)] * 2,
             out_specs=(anywhere, anywhere),
             scratch_shapes=[dma((2,))],
-            compiler_params=pltpu.CompilerParams(vmem_limit_bytes=60 * 2**20),
+            compiler_params=pltpu.CompilerParams(vmem_limit_bytes=4 * 2**20),
         )(*results)
 
     return jax.shard_map(

time: 34.1 us -> 28.8 us (0.84)
  Pallas kernels: 32.6 us -> 27.3 us
    pallas_call x1, Pallas kernels: 5.34 us -> 0.68 us  [per_device(): pl.pallas_call(hand_over, out_shape=outs, in_specs=[pl.BlockSpec(memory_s...]
    pallas_call x1, Pallas kernels: 27.3 us -> 26.6 us  [per_device(): pl.pallas_call(functools.partial(kernel, n), out_shape=outs, in_specs=[an...]
where the time goes in v3:
time: 28.8 us; the launch traced here: 28.6 us
  Pallas kernels  27.3 us (95%)
  between operations  1.29 us (4%)
    pallas_call x1, Pallas kernels, per_device(): pl.pallas_call(functools.partial(kernel, n), out_shape=outs, in_specs=[an...  26.6 us
    pallas_call x1, Pallas kernels, per_device(): pl.pallas_call(hand_over, out_shape=outs, in_specs=[pl.BlockSpec(memory_s...  0.68 us

profile of v3, /device:TPU:0, one launch (start us, length us, event | category | flops | bytes accessed | tf_op | source)
XLA Modules:
  0.0 28.6 jit_solution(6967699053266559215)
XLA Ops:
  1.3 26.6 %shard_map.77 = (f32[128,256]{1,0:T(8,128)S(1)}, f32[4,512]{1,0:T(4,128)S(1)}) custom-call(f32[16,1024]{1,0:T(8,128)} %ds_hbm.1, f32[128,1024]{1,0:T(8,128)} %cen_hbm.1, f32[128,256]{1,0:T(8,128)} %w_hbm.1, s32[2,4]{1,0:T(2,128)} %idx_hbm.1, f32[2,4,512]{2,1,0:T(4,128)} %tgt_hbm.1, f32[1]{0:T(128)S(6)} %copy.8.gam_ref), custom_call_target="tpu_custom_call" | custom-call | tf_op jit(solution)/shard_map/pallas_call | solution.py:280
  27.9 0.7 %shard_map.78 = (f32[128,256]{1,0:T(8,128)}, f32[4,512]{1,0:T(4,128)}) custom-call(f32[128,256]{1,0:T(8,128)S(1)} %get-tuple-element.4.w_in, f32[4,512]{1,0:T(4,128)S(1)} %get-tuple-element.5.res_in), custom_call_target="tpu_custom_call" | custom-call | tf_op jit(solution)/shard_map/pallas_call | solution.py:308

commit v4 on v3

--- a/solution.py
+++ b/solution.py
@@ -22,7 +22,9 @@
 def dot3(a, b, dims=NN):
     (ah, al), (bh, bl) = a, b
     dot = functools.partial(lax.dot_general, dimension_numbers=dims, preferred_element_type=jnp.float32)
-    return dot(ah, bh) + (dot(ah, bl) + dot(al, bh))
+    both = dot(jnp.concatenate([ah, al], axis=0), bh)
+    height = ah.shape[0]
+    return both[:height] + (dot(ah, bl) + both[height:])
 
 
 def each(lo, hi, body):
@@ -36,8 +38,8 @@
 def kernel(
     n, ds_hbm, cen_hbm, w_hbm, idx_hbm, tgt_hbm, gam_ref, w_out, res_out,
     ds_ref, cen_ref, w_ref, idx_ref, tgt_ref,
-    xbuf, kbuf, tsib, tplace, part, rs_in, allv, res_s, rsend, rrecv,
-    in_s, x_ss, x_rs, f_ss, f_rs, p_ss, p_rs, a_ss, a_rs, s_ss, s_rs,
+    xbuf, kbuf, tsib, tplace, part, rs_in, partq, rs_inq, allv, res_s, rsend, rrecv,
+    in_s, x_ss, x_rs, f_ss, f_rs, p_ss, p_rs, q_ss, q_rs, a_ss, a_rs, s_ss, s_rs,
 ):
     f32 = jnp.float32
     c, r = lax.axis_index("center"), lax.axis_index("row")
@@ -47,12 +49,11 @@
     place = side * half + h
     steps, rows = idx_ref.shape
     slot = steps * rows
-    chunks = 2 * n
-    batch = rows * chunks
+    batch = 2 * rows * n
     cols = w_ref.shape[1]
     ncen = cen_ref.shape[0]
     rate = 0.5 / batch
-    fold, rp, rg, pw, gw = sizes(n, batch, steps, cols)
+    fold, rg, pw, gw = sizes(n, batch, cols)
 
     ins = [
         pltpu.make_async_copy(src, dst, in_s.at[i])
@@ -137,51 +138,71 @@
     k_copy(1, side).start()
 
     t_copy.wait()
-    chunk_id = lax.broadcasted_iota(jnp.int32, (chunks, cols), 0)
-    for b in range(steps):
-        mine, other = tgt_ref[b, :, own_cols], tsib[b]
-        for i in range(rows):
-            j = b * rows + i
-            placed = jnp.where(chunk_id == r * n + place, mine[i : i + 1, :], 0.0)
-            placed = jnp.where(chunk_id == sib * n + place, other[i : i + 1, :], placed)
-            tplace[pl.ds(j * chunks, chunks), :] = placed
+    place_id = lax.broadcasted_iota(jnp.int32, (n, cols), 0)
+    for j in range(slot):
+        b, i = divmod(j, rows)
+        tplace[0, j * n : (j + 1) * n, :] = jnp.where(place_id == place, tgt_ref[b, i : i + 1, own_cols], 0.0)
+        tplace[1, j * n : (j + 1) * n, :] = jnp.where(place_id == place, tsib[b, i : i + 1, :], 0.0)
 
     each(0, half, lambda e: f_copy(e).wait_recv())
     each(0, count // step, lambda s: kernel_rows(1 - side, s))
     k_copy(2, 1 - side).start()
+
+    def core_rows(core):
+        return jnp.concatenate(
+            [kbuf[pl.ds(core * (n * slot) + j, n, stride=slot), :] for j in range(slot)], axis=0
+        )
+
+    def predict(core, which):
+        return dot3(split(core_rows(core)), w2) - tplace[which]
+
+    def put(ref, values, at, size):
+        for l in range(values.shape[1] // LANES):
+            for o in range(n):
+                ref[o, at + l * size : at + (l + 1) * size, :] = values[
+                    o * size : (o + 1) * size, l * LANES : (l + 1) * LANES
+                ]
+
+    def p_copy(d):
+        return copy(part.at[lax.rem(c + d, n)], rs_in.at[d], p_ss.at[d], p_rs.at[d], to(d))
+
+    def q_copy(d):
+        return copy(partq.at[lax.rem(c + d, n)], rs_inq.at[d], q_ss.at[d], q_rs.at[d], to(d))
+
+    put(part, predict(r, 0), 0, slot)
+    each(1, n, lambda d: p_copy(d).start())
+
     k_copy(1, side).wait()
     k_copy(2, 1 - side).wait()
-
-    k_all = jnp.concatenate([kbuf[pl.ds(j, chunks, stride=slot), :] for j in range(slot)], axis=0)
-    kh, kl = split(k_all)
-    k0 = (jnp.concatenate([kh[:batch]] * fold, axis=0), jnp.concatenate([kl[:batch]] * fold, axis=0))
-
-    blocks = max(1, n // UNROLL)
-    per = n // blocks
-    for s in range(blocks):
-        lo, hi = s * per * rp, (s + 1) * per * rp
-        p = dot3((kh[lo:hi], kl[lo:hi]), w2) - tplace[lo:hi, :]
-        lo, hi = batch + s * per * rg * fold, batch + (s + 1) * per * rg * fold
-        g = fold_rows(dot3((kh[lo:hi], kl[lo:hi]), k0, NT), fold, batch)
-        for o in range(per):
-            for l in range(pw):
-                part[s * per + o, l * rp : (l + 1) * rp, :] = p[o * rp : (o + 1) * rp, l * LANES : (l + 1) * LANES]
-            for l in range(gw):
-                at = pw * rp + l * rg
-                part[s * per + o, at : at + rg, :] = g[o * rg : (o + 1) * rg, l * LANES : (l + 1) * LANES]
-
-    def p_copy(d):
-        return copy(part.at[lax.rem(c + d, n)], rs_in.at[d], p_ss.at[d], p_rs.at[d], to(d))
-
-    each(1, n, lambda d: p_copy(d).start())
-    k_t = split(jnp.transpose(k_all))
-    allv[c] = part[c]
+    put(partq, predict(sib, 1), 0, slot)
+    kernels = [core_rows(core) for core in range(2)]
+    k_0 = jnp.concatenate([v[: rows * n] for v in kernels], axis=0)
+    k_1 = jnp.concatenate([v[rows * n :] for v in kernels], axis=0)
+    k0h, k0l = split(k_0)
+    k0f = (jnp.concatenate([k0h] * fold, axis=0), jnp.concatenate([k0l] * fold, axis=0))
+    put(partq, fold_rows(dot3(split(k_1), k0f, NT), fold, batch), pw * slot, rg)
+    each(1, n, lambda d: q_copy(d).start())
+
+    k_t = split(jnp.transpose(jnp.concatenate([k_0, k_1], axis=0)))
+    core_at = [pl.multiple_of(core * (pw * slot), slot) for core in (r, sib)]
+    own_at, sib_at = (pl.ds(at, pw * slot) for at in core_at)
+    g_at = pl.ds(2 * pw * slot, gw * rg)
+    q_at, qg_at = pl.ds(0, pw * slot), pl.ds(pw * slot, gw * rg)
+    allv[c, own_at, :] = part[c]
+    allv[c, sib_at, :] = partq[c, q_at, :]
+    allv[c, g_at, :] = partq[c, qg_at, :]
 
     def add(d):
         p_copy(d).wait_recv()
-        allv[c] += rs_in[d]
+        allv[c, own_at, :] += rs_in[d]
+
+    def addq(d):
+        q_copy(d).wait_recv()
+        allv[c, sib_at, :] += rs_inq[d, q_at, :]
+        allv[c, g_at, :] += rs_inq[d, qg_at, :]
 
     each(1, n, add)
+    each(1, n, addq)
 
     def a_copy(d):
         return copy(allv.at[c], allv.at[c], a_ss.at[d], a_rs.at[d], to(d))
@@ -189,26 +210,27 @@
     each(1, n, lambda d: a_copy(d).start())
     each(1, n, lambda d: a_copy(d).wait_recv())
 
-    def whole(at, size, width):
+    def take(at, size, width, owners):
         pieces = [
-            jnp.concatenate([allv[o, at + l * size : at + (l + 1) * size, :] for o in range(n)], axis=0)
+            jnp.concatenate([allv[o, at + l * size : at + (l + 1) * size, :] for o in owners], axis=0)
             for l in range(width)
         ]
         return pieces[0] if width == 1 else jnp.concatenate(pieces, axis=1)
 
-    a = whole(0, rp, pw)
-    g = unfold_rows(whole(pw * rp, rg, gw), fold, batch)
-    res0 = a[:batch]
-    res0h, res0l = split(res0)
+    def both_cores(owners):
+        return jnp.concatenate([take(core * (pw * slot), slot, pw, owners) for core in range(2)], axis=0)
+
+    g = unfold_rows(take(2 * pw * slot, rg, gw, range(n)), fold, batch)
+    res0h, res0l = split(both_cores(range(n // 2)))
     res0f = (jnp.concatenate([res0h] * fold, axis=0), jnp.concatenate([res0l] * fold, axis=0))
-    res1 = a[batch:] - rate * dot3(split(g), res0f)
+    res1 = both_cores(range(n // 2, n)) - rate * dot3(split(g), res0f)
     res_s[...] = res1
     for i in range(rows):
-        rsend[i : i + 1, :] = res_s[pl.ds(i * chunks + sib * n + place, 1), :]
+        rsend[i : i + 1, :] = res_s[pl.ds((sib * rows + i) * n + place, 1), :]
     r_copy = copy(rsend, rrecv, s_ss.at[3], s_rs.at[3], to_sib)
     r_copy.start()
     for i in range(rows):
-        res_out[i : i + 1, own_cols] = res_s[pl.ds(i * chunks + r * n + place, 1), :]
+        res_out[i : i + 1, own_cols] = res_s[pl.ds((r * rows + i) * n + place, 1), :]
     res1h, res1l = split(res1)
     res = (jnp.concatenate([res0h, res1h], axis=0), jnp.concatenate([res0l, res1l], axis=0))
     w_out[...] = w_ref[...] - rate * dot3(k_t, res)
@@ -217,6 +239,7 @@
 
     def drain(d):
         p_copy(d).wait_send()
+        q_copy(d).wait_send()
         a_copy(d).wait_send()
 
     each(1, n, drain)
@@ -224,9 +247,9 @@
     each(0, half, lambda e: f_copy(e).wait_send())
 
 
-def sizes(n, batch, steps, cols):
+def sizes(n, batch, cols):
     fold = max(1, LANES // batch)
-    return fold, steps * batch // n, batch // fold // n, cols // LANES, pl.cdiv(batch, LANES)
+    return fold, batch // fold // n, cols // LANES, pl.cdiv(batch, LANES)
 
 
 def fold_rows(g, fold, batch):
@@ -267,8 +290,8 @@
         slot, feats = steps * rows, dataset.shape[1]
         ncen, cols = weights.shape
         total, batch = slot * 2 * n, rows * 2 * n
-        fold, rp, rg, pw, gw = sizes(n, batch, steps, cols)
-        height = pw * rp + gw * rg
+        fold, rg, pw, gw = sizes(n, batch, cols)
+        height, extra = pw * slot, gw * rg
         half = n // 2
         vm = pltpu.VMEM
         dma = pltpu.SemaphoreType.DMA
@@ -288,15 +311,17 @@
                 vm((n, slot, feats), f32),
                 vm((2 * n * slot, ncen), f32),
                 vm((steps, rows, cols), f32),
-                vm((total, cols), f32),
+                vm((2, total // 2, cols), f32),
                 vm((n, height, LANES), f32),
                 vm((n, height, LANES), f32),
-                vm((n, height, LANES), f32),
+                vm((n, height + extra, LANES), f32),
+                vm((n, height + extra, LANES), f32),
+                vm((n, 2 * height + extra, LANES), f32),
                 vm((batch, cols), f32),
                 vm((rows, cols), f32),
                 vm((rows, cols), f32),
                 dma((5,)), dma((half,)), dma((half,)), dma((half,)), dma((half,)),
-                dma((n,)), dma((n,)), dma((n,)), dma((n,)), dma((4,)), dma((4,)),
+                dma((n,)), dma((n,)), dma((n,)), dma((n,)), dma((n,)), dma((n,)), dma((4,)), dma((4,)),
             ],
             compiler_params=pltpu.CompilerParams(
                 collective_id=0, has_side_effects=True, vmem_limit_bytes=min(56, 8 + 3 * n) * 2**20

time: 28.8 us -> 27.8 us (0.965)
  Pallas kernels: 27.3 us -> 26.3 us
    pallas_call x1, Pallas kernels: 26.6 us -> 25.6 us  [per_device(): pl.pallas_call(functools.partial(kernel, n), out_shape=outs, in_specs=[an...]
where the time goes in v4:
time: 27.8 us; the launch traced here: 27.6 us
  Pallas kernels  26.3 us (95%)
  between operations  1.29 us (5%)
    pallas_call x1, Pallas kernels, per_device(): pl.pallas_call(functools.partial(kernel, n), out_shape=outs, in_specs=[an...  25.6 us
    pallas_call x1, Pallas kernels, per_device(): pl.pallas_call(hand_over, out_shape=outs, in_specs=[pl.BlockSpec(memory_s...  0.68 us

profile of v4, /device:TPU:0, one launch (start us, length us, event | category | flops | bytes accessed | tf_op | source)
XLA Modules:
  0.0 27.6 jit_solution(2250489386209605735)
XLA Ops:
  1.3 25.6 %shard_map.77 = (f32[128,256]{1,0:T(8,128)S(1)}, f32[4,512]{1,0:T(4,128)S(1)}) custom-call(f32[16,1024]{1,0:T(8,128)} %ds_hbm.1, f32[128,1024]{1,0:T(8,128)} %cen_hbm.1, f32[128,256]{1,0:T(8,128)} %w_hbm.1, s32[2,4]{1,0:T(2,128)} %idx_hbm.1, f32[2,4,512]{2,1,0:T(4,128)} %tgt_hbm.1, f32[1]{0:T(128)S(6)} %copy.8.gam_ref), custom_call_target="tpu_custom_call" | custom-call | tf_op jit(solution)/shard_map/pallas_call | solution.py:303
  26.9 0.7 %shard_map.78 = (f32[128,256]{1,0:T(8,128)}, f32[4,512]{1,0:T(4,128)}) custom-call(f32[128,256]{1,0:T(8,128)S(1)} %get-tuple-element.4.w_in, f32[4,512]{1,0:T(4,128)S(1)} %get-tuple-element.5.res_in), custom_call_target="tpu_custom_call" | custom-call | tf_op jit(solution)/shard_map/pallas_call | solution.py:333

commit v5 on v4

--- a/solution.py
+++ b/solution.py
@@ -38,8 +38,8 @@
 def kernel(
     n, ds_hbm, cen_hbm, w_hbm, idx_hbm, tgt_hbm, gam_ref, w_out, res_out,
     ds_ref, cen_ref, w_ref, idx_ref, tgt_ref,
-    xbuf, kbuf, tsib, tplace, part, rs_in, partq, rs_inq, allv, res_s, rsend, rrecv,
-    in_s, x_ss, x_rs, f_ss, f_rs, p_ss, p_rs, q_ss, q_rs, a_ss, a_rs, s_ss, s_rs,
+    xbuf, kbuf, tsib, tplace, part, rs_in, partq, rs_inq, sums, sumsq, res_s, rsend, rrecv,
+    in_s, x_ss, x_rs, f_ss, f_rs, p_ss, p_rs, q_ss, q_rs, a_ss, a_rs, b_ss, b_rs, s_ss, s_rs,
 ):
     f32 = jnp.float32
     c, r = lax.axis_index("center"), lax.axis_index("row")
@@ -153,8 +153,8 @@
             [kbuf[pl.ds(core * (n * slot) + j, n, stride=slot), :] for j in range(slot)], axis=0
         )
 
-    def predict(core, which):
-        return dot3(split(core_rows(core)), w2) - tplace[which]
+    def predict(which):
+        return dot3(split(kernels[which]), w2) - tplace[which]
 
     def put(ref, values, at, size):
         for l in range(values.shape[1] // LANES):
@@ -169,13 +169,14 @@
     def q_copy(d):
         return copy(partq.at[lax.rem(c + d, n)], rs_inq.at[d], q_ss.at[d], q_rs.at[d], to(d))
 
-    put(part, predict(r, 0), 0, slot)
+    kernels = [core_rows(r)]
+    put(part, predict(0), 0, slot)
     each(1, n, lambda d: p_copy(d).start())
 
     k_copy(1, side).wait()
     k_copy(2, 1 - side).wait()
-    put(partq, predict(sib, 1), 0, slot)
-    kernels = [core_rows(core) for core in range(2)]
+    kernels.append(core_rows(sib))
+    put(partq, predict(1), 0, slot)
     k_0 = jnp.concatenate([v[: rows * n] for v in kernels], axis=0)
     k_1 = jnp.concatenate([v[rows * n :] for v in kernels], axis=0)
     k0h, k0l = split(k_0)
@@ -184,53 +185,51 @@
     each(1, n, lambda d: q_copy(d).start())
 
     k_t = split(jnp.transpose(jnp.concatenate([k_0, k_1], axis=0)))
-    core_at = [pl.multiple_of(core * (pw * slot), slot) for core in (r, sib)]
-    own_at, sib_at = (pl.ds(at, pw * slot) for at in core_at)
-    g_at = pl.ds(2 * pw * slot, gw * rg)
-    q_at, qg_at = pl.ds(0, pw * slot), pl.ds(pw * slot, gw * rg)
-    allv[c, own_at, :] = part[c]
-    allv[c, sib_at, :] = partq[c, q_at, :]
-    allv[c, g_at, :] = partq[c, qg_at, :]
+    sums[c] = part[c]
+    sumsq[c] = partq[c]
 
     def add(d):
         p_copy(d).wait_recv()
-        allv[c, own_at, :] += rs_in[d]
+        sums[c] += rs_in[d]
 
     def addq(d):
         q_copy(d).wait_recv()
-        allv[c, sib_at, :] += rs_inq[d, q_at, :]
-        allv[c, g_at, :] += rs_inq[d, qg_at, :]
+        sumsq[c] += rs_inq[d]
+
+    def a_copy(d):
+        return copy(sums.at[c], sums.at[c], a_ss.at[d], a_rs.at[d], to(d))
+
+    def b_copy(d):
+        return copy(sumsq.at[c], sumsq.at[c], b_ss.at[d], b_rs.at[d], to(d))
 
     each(1, n, add)
+    each(1, n, lambda d: a_copy(d).start())
     each(1, n, addq)
-
-    def a_copy(d):
-        return copy(allv.at[c], allv.at[c], a_ss.at[d], a_rs.at[d], to(d))
-
-    each(1, n, lambda d: a_copy(d).start())
+    each(1, n, lambda d: b_copy(d).start())
     each(1, n, lambda d: a_copy(d).wait_recv())
-
-    def take(at, size, width, owners):
+    each(1, n, lambda d: b_copy(d).wait_recv())
+
+    def take(ref, at, size, width, owners):
         pieces = [
-            jnp.concatenate([allv[o, at + l * size : at + (l + 1) * size, :] for o in owners], axis=0)
+            jnp.concatenate([ref[o, at + l * size : at + (l + 1) * size, :] for o in owners], axis=0)
             for l in range(width)
         ]
         return pieces[0] if width == 1 else jnp.concatenate(pieces, axis=1)
 
     def both_cores(owners):
-        return jnp.concatenate([take(core * (pw * slot), slot, pw, owners) for core in range(2)], axis=0)
-
-    g = unfold_rows(take(2 * pw * slot, rg, gw, range(n)), fold, batch)
+        return jnp.concatenate([take(ref, 0, slot, pw, owners) for ref in (sums, sumsq)], axis=0)
+
+    g = unfold_rows(take(sumsq, pw * slot, rg, gw, range(n)), fold, batch)
     res0h, res0l = split(both_cores(range(n // 2)))
     res0f = (jnp.concatenate([res0h] * fold, axis=0), jnp.concatenate([res0l] * fold, axis=0))
     res1 = both_cores(range(n // 2, n)) - rate * dot3(split(g), res0f)
     res_s[...] = res1
     for i in range(rows):
-        rsend[i : i + 1, :] = res_s[pl.ds((sib * rows + i) * n + place, 1), :]
+        rsend[i : i + 1, :] = res_s[pl.ds((rows + i) * n + place, 1), :]
     r_copy = copy(rsend, rrecv, s_ss.at[3], s_rs.at[3], to_sib)
     r_copy.start()
     for i in range(rows):
-        res_out[i : i + 1, own_cols] = res_s[pl.ds((r * rows + i) * n + place, 1), :]
+        res_out[i : i + 1, own_cols] = res_s[pl.ds(i * n + place, 1), :]
     res1h, res1l = split(res1)
     res = (jnp.concatenate([res0h, res1h], axis=0), jnp.concatenate([res0l, res1l], axis=0))
     w_out[...] = w_ref[...] - rate * dot3(k_t, res)
@@ -241,6 +240,7 @@
         p_copy(d).wait_send()
         q_copy(d).wait_send()
         a_copy(d).wait_send()
+        b_copy(d).wait_send()
 
     each(1, n, drain)
     each(1, half, lambda e: x_copy(e).wait_send())
@@ -316,12 +316,13 @@
                 vm((n, height, LANES), f32),
                 vm((n, height + extra, LANES), f32),
                 vm((n, height + extra, LANES), f32),
-                vm((n, 2 * height + extra, LANES), f32),
+                vm((n, height, LANES), f32),
+                vm((n, height + extra, LANES), f32),
                 vm((batch, cols), f32),
                 vm((rows, cols), f32),
                 vm((rows, cols), f32),
                 dma((5,)), dma((half,)), dma((half,)), dma((half,)), dma((half,)),
-                dma((n,)), dma((n,)), dma((n,)), dma((n,)), dma((n,)), dma((n,)), dma((4,)), dma((4,)),
+                dma((n,)), dma((n,)), dma((n,)), dma((n,)), dma((n,)), dma((n,)), dma((n,)), dma((n,)), dma((4,)), dma((4,)),
             ],
             compiler_params=pltpu.CompilerParams(
                 collective_id=0, has_side_effects=True, vmem_limit_bytes=min(56, 8 + 3 * n) * 2**20

time: 27.8 us -> 27.6 us (level)
  no operation moved by 1% of the time
where the time goes in v5:
time: 27.6 us; the launch traced here: 27.5 us
  Pallas kernels  26.2 us (95%)
  between operations  1.29 us (5%)
    pallas_call x1, Pallas kernels, per_device(): pl.pallas_call(functools.partial(kernel, n), out_shape=outs, in_specs=[an...  25.5 us
    pallas_call x1, Pallas kernels, per_device(): pl.pallas_call(hand_over, out_shape=outs, in_specs=[pl.BlockSpec(memory_s...  0.68 us

profile of v5, /device:TPU:0, one launch (start us, length us, event | category | flops | bytes accessed | tf_op | source)
XLA Modules:
  0.0 27.5 jit_solution(6960595803455942718)
XLA Ops:
  1.3 25.5 %shard_map.77 = (f32[128,256]{1,0:T(8,128)S(1)}, f32[4,512]{1,0:T(4,128)S(1)}) custom-call(f32[16,1024]{1,0:T(8,128)} %ds_hbm.1, f32[128,1024]{1,0:T(8,128)} %cen_hbm.1, f32[128,256]{1,0:T(8,128)} %w_hbm.1, s32[2,4]{1,0:T(2,128)} %idx_hbm.1, f32[2,4,512]{2,1,0:T(4,128)} %tgt_hbm.1, f32[1]{0:T(128)S(6)} %copy.8.gam_ref), custom_call_target="tpu_custom_call" | custom-call | tf_op jit(solution)/shard_map/pallas_call | solution.py:303
  26.8 0.7 %shard_map.78 = (f32[128,256]{1,0:T(8,128)}, f32[4,512]{1,0:T(4,128)}) custom-call(f32[128,256]{1,0:T(8,128)S(1)} %get-tuple-element.4.w_in, f32[4,512]{1,0:T(4,128)S(1)} %get-tuple-element.5.res_in), custom_call_target="tpu_custom_call" | custom-call | tf_op jit(solution)/shard_map/pallas_call | solution.py:334

commit v6 on v5

--- a/solution.py
+++ b/solution.py
@@ -21,10 +21,12 @@
 
 def dot3(a, b, dims=NN):
     (ah, al), (bh, bl) = a, b
-    dot = functools.partial(lax.dot_general, dimension_numbers=dims, preferred_element_type=jnp.float32)
-    both = dot(jnp.concatenate([ah, al], axis=0), bh)
-    height = ah.shape[0]
-    return both[:height] + (dot(ah, bl) + both[height:])
+    return lax.dot_general(
+        jnp.concatenate([ah, al, ah], axis=1),
+        jnp.concatenate([bh, bh, bl], axis=dims[0][1][0]),
+        dims,
+        preferred_element_type=jnp.float32,
+    )
 
 
 def each(lo, hi, body):
@@ -104,10 +106,9 @@
     t_copy.start()
 
     ins[3].wait()
-    cen = cen_ref[...]
-    cen2 = split(cen)
-    csq = jnp.sum(cen * cen, axis=1, keepdims=True)
-    csq = jnp.transpose(jnp.broadcast_to(csq, (ncen, ncen)))[0:1, :]
+    cen = jnp.transpose(cen_ref[...])
+    cen2 = jnp.concatenate(split(cen), axis=1)
+    csq = jnp.sum(cen * cen, axis=0, keepdims=True)
     ins[4].wait()
     w2 = split(w_ref[...])
     gamma = gam_ref[0]
@@ -125,7 +126,8 @@
         first = pl.multiple_of(which * count + s * step, slot)
         x = xbuf[pl.ds(which * half + s * (step // slot), step // slot)].reshape(step, xbuf.shape[2])
         xsq = jnp.sum(x * x, axis=1, keepdims=True)
-        cross = dot3(split(x), cen2, NT)
+        quad = jnp.dot(jnp.concatenate(split(x), axis=0), cen2, preferred_element_type=f32)
+        cross = quad[:step, :ncen] + (quad[:step, ncen:] + quad[step:, :ncen] + quad[step:, ncen:])
         kbuf[pl.ds(pl.multiple_of(r * (n * slot) + first, slot), step), :] = jnp.exp(
             -gamma * (xsq + csq - 2.0 * cross)
         )

time: 27.6 us -> 27.5 us (level)
  no operation moved by 1% of the time
where the time goes in v6:
time: 27.5 us; the launch traced here: 27.3 us
  Pallas kernels  26 us (95%)
  between operations  1.29 us (5%)
    pallas_call x1, Pallas kernels, per_device(): pl.pallas_call(functools.partial(kernel, n), out_shape=outs, in_specs=[an...  25.3 us
    pallas_call x1, Pallas kernels, per_device(): pl.pallas_call(hand_over, out_shape=outs, in_specs=[pl.BlockSpec(memory_s...  0.68 us

profile of v6, /device:TPU:0, one launch (start us, length us, event | category | flops | bytes accessed | tf_op | source)
XLA Modules:
  0.0 27.3 jit_solution(5908774342434254049)
XLA Ops:
  1.3 25.3 %shard_map.77 = (f32[128,256]{1,0:T(8,128)S(1)}, f32[4,512]{1,0:T(4,128)S(1)}) custom-call(f32[16,1024]{1,0:T(8,128)} %ds_hbm.1, f32[128,1024]{1,0:T(8,128)} %cen_hbm.1, f32[128,256]{1,0:T(8,128)} %w_hbm.1, s32[2,4]{1,0:T(2,128)} %idx_hbm.1, f32[2,4,512]{2,1,0:T(4,128)} %tgt_hbm.1, f32[1]{0:T(128)S(6)} %copy.8.gam_ref), custom_call_target="tpu_custom_call" | custom-call | tf_op jit(solution)/shard_map/pallas_call | solution.py:305
  26.6 0.7 %shard_map.78 = (f32[128,256]{1,0:T(8,128)}, f32[4,512]{1,0:T(4,128)}) custom-call(f32[128,256]{1,0:T(8,128)S(1)} %get-tuple-element.4.w_in, f32[4,512]{1,0:T(4,128)S(1)} %get-tuple-element.5.res_in), custom_call_target="tpu_custom_call" | custom-call | tf_op jit(solution)/shard_map/pallas_call | solution.py:336

commit v7 on v6

--- a/solution.py
+++ b/solution.py
@@ -55,7 +55,7 @@
     cols = w_ref.shape[1]
     ncen = cen_ref.shape[0]
     rate = 0.5 / batch
-    fold, rg, pw, gw = sizes(n, batch, cols)
+    first, owners, fold, rp, rg, pw, gw = sizes(n, batch, cols, steps)
 
     ins = [
         pltpu.make_async_copy(src, dst, in_s.at[i])
@@ -63,18 +63,16 @@
             [(idx_hbm, idx_ref), (ds_hbm, ds_ref), (tgt_hbm, tgt_ref), (cen_hbm, cen_ref), (w_hbm, w_ref)]
         )
     ]
+    barrier = pltpu.get_barrier_semaphore()
+
+    def to(d):
+        return {"center": lax.rem(c + d, n), "row": r}
+
+    to_sib = {"center": c, "row": sib}
+    each(1, n, lambda d: pl.semaphore_signal(barrier, inc=1, device_id=to(d), device_id_type=MESH))
+    pl.semaphore_signal(barrier, inc=1, device_id=to_sib, device_id_type=MESH)
     for one in ins:
         one.start()
-
-    barrier = pltpu.get_barrier_semaphore()
-
-    def to(d):
-        return {"center": lax.rem(c + d, n), "row": r}
-
-    to_sib = {"center": c, "row": sib}
-    to_pair = {"center": 2 * h + 1 - side, "row": r}
-    each(1, n, lambda d: pl.semaphore_signal(barrier, inc=1, device_id=to(d), device_id_type=MESH))
-    pl.semaphore_signal(barrier, inc=1, device_id=to_sib, device_id_type=MESH)
 
     def copy(src, dst, ss, rs, peer):
         return pltpu.make_async_remote_copy(
@@ -86,7 +84,6 @@
     for b in range(steps):
         for i in range(rows):
             xbuf[place, pl.ds(b * rows + i, 1), :] = ds_ref[pl.ds(idx_ref[b, i], 1), :]
-    ins[2].wait()
 
     pl.semaphore_wait(barrier, n)
 
@@ -95,14 +92,15 @@
         return copy(xbuf.at[place], xbuf.at[place], x_ss.at[e], x_rs.at[e], peer)
 
     def f_copy(e):
-        at = side * half + lax.rem(h + half - e, half)
-        return copy(xbuf.at[at], xbuf.at[at], f_ss.at[e], f_rs.at[e], to_pair)
+        peer = {"center": 2 * lax.rem(h + e, half) + 1 - side, "row": r}
+        return copy(xbuf.at[place], xbuf.at[place], f_ss.at[e], f_rs.at[e], peer)
 
     each(1, half, lambda e: x_copy(e).start())
-    f_copy(0).start()
+    each(0, half, lambda e: f_copy(e).start())
     sib_cols = pl.ds(pl.multiple_of(sib * cols, LANES), cols)
     own_cols = pl.ds(pl.multiple_of(r * cols, LANES), cols)
     t_copy = copy(tgt_ref.at[:, :, sib_cols], tsib, s_ss.at[0], s_rs.at[0], to_sib)
+    ins[2].wait()
     t_copy.start()
 
     ins[3].wait()
@@ -113,11 +111,7 @@
     w2 = split(w_ref[...])
     gamma = gam_ref[0]
 
-    def pass_on(e):
-        x_copy(e).wait_recv()
-        f_copy(e).start()
-
-    each(1, half, pass_on)
+    each(1, half, lambda e: x_copy(e).wait_recv())
 
     count = half * slot
     step = min(count, UNROLL * slot)
@@ -160,71 +154,96 @@
 
     def put(ref, values, at, size):
         for l in range(values.shape[1] // LANES):
-            for o in range(n):
+            for o in range(owners):
                 ref[o, at + l * size : at + (l + 1) * size, :] = values[
                     o * size : (o + 1) * size, l * LANES : (l + 1) * LANES
                 ]
 
-    def p_copy(d):
-        return copy(part.at[lax.rem(c + d, n)], rs_in.at[d], p_ss.at[d], p_rs.at[d], to(d))
-
-    def q_copy(d):
-        return copy(partq.at[lax.rem(c + d, n)], rs_inq.at[d], q_ss.at[d], q_rs.at[d], to(d))
+    def owns(device):
+        return jnp.logical_and(device >= first, device < first + owners)
+
+    def p_copy(d, at):
+        return copy(part.at[at], rs_in.at[d], p_ss.at[d], p_rs.at[d], to(d))
+
+    def q_copy(d, at):
+        return copy(partq.at[at], rs_inq.at[d], q_ss.at[d], q_rs.at[d], to(d))
+
+    def to_owners(body):
+        def one(d):
+            at = lax.rem(c + d, n)
+            pl.when(owns(at))(lambda: body(d, at - first))
+
+        each(1, n, one)
 
     kernels = [core_rows(r)]
-    put(part, predict(0), 0, slot)
-    each(1, n, lambda d: p_copy(d).start())
+    put(part, predict(0), 0, rp)
+    to_owners(lambda d, at: p_copy(d, at).start())
 
     k_copy(1, side).wait()
     k_copy(2, 1 - side).wait()
     kernels.append(core_rows(sib))
-    put(partq, predict(1), 0, slot)
+    put(partq, predict(1), 0, rp)
     k_0 = jnp.concatenate([v[: rows * n] for v in kernels], axis=0)
     k_1 = jnp.concatenate([v[rows * n :] for v in kernels], axis=0)
     k0h, k0l = split(k_0)
     k0f = (jnp.concatenate([k0h] * fold, axis=0), jnp.concatenate([k0l] * fold, axis=0))
-    put(partq, fold_rows(dot3(split(k_1), k0f, NT), fold, batch), pw * slot, rg)
-    each(1, n, lambda d: q_copy(d).start())
+    put(partq, fold_rows(dot3(split(k_1), k0f, NT), fold, batch), pw * rp, rg)
+    to_owners(lambda d, at: q_copy(d, at).start())
 
     k_t = split(jnp.transpose(jnp.concatenate([k_0, k_1], axis=0)))
-    sums[c] = part[c]
-    sumsq[c] = partq[c]
-
-    def add(d):
-        p_copy(d).wait_recv()
-        sums[c] += rs_in[d]
-
-    def addq(d):
-        q_copy(d).wait_recv()
-        sumsq[c] += rs_inq[d]
-
-    def a_copy(d):
-        return copy(sums.at[c], sums.at[c], a_ss.at[d], a_rs.at[d], to(d))
-
-    def b_copy(d):
-        return copy(sumsq.at[c], sumsq.at[c], b_ss.at[d], b_rs.at[d], to(d))
-
-    each(1, n, add)
-    each(1, n, lambda d: a_copy(d).start())
-    each(1, n, addq)
-    each(1, n, lambda d: b_copy(d).start())
-    each(1, n, lambda d: a_copy(d).wait_recv())
-    each(1, n, lambda d: b_copy(d).wait_recv())
-
-    def take(ref, at, size, width, owners):
+
+    def gathered(ref, at, ss, rs, d):
+        return copy(ref.at[at - first], ref.at[at - first], ss.at[d], rs.at[d], to(d))
+
+    def a_copy(at, d):
+        return gathered(sums, at, a_ss, a_rs, d)
+
+    def b_copy(at, d):
+        return gathered(sumsq, at, b_ss, b_rs, d)
+
+    @pl.when(owns(c))
+    def _():
+        me = c - first
+        sums[me] = part[me]
+        sumsq[me] = partq[me]
+
+        def add(d):
+            p_copy(d, me).wait_recv()
+            sums[me] += rs_in[d]
+
+        def addq(d):
+            q_copy(d, me).wait_recv()
+            sumsq[me] += rs_inq[d]
+
+        each(1, n, add)
+        each(1, n, lambda d: a_copy(c, d).start())
+        each(1, n, addq)
+        each(1, n, lambda d: b_copy(c, d).start())
+
+    def arrive(d):
+        at = lax.rem(c + n - d, n)
+
+        @pl.when(owns(at))
+        def _():
+            a_copy(at, d).wait_recv()
+            b_copy(at, d).wait_recv()
+
+    each(1, n, arrive)
+
+    def take(ref, at, size, width, which):
         pieces = [
-            jnp.concatenate([ref[o, at + l * size : at + (l + 1) * size, :] for o in owners], axis=0)
+            jnp.concatenate([ref[o, at + l * size : at + (l + 1) * size, :] for o in which], axis=0)
             for l in range(width)
         ]
         return pieces[0] if width == 1 else jnp.concatenate(pieces, axis=1)
 
-    def both_cores(owners):
-        return jnp.concatenate([take(ref, 0, slot, pw, owners) for ref in (sums, sumsq)], axis=0)
-
-    g = unfold_rows(take(sumsq, pw * slot, rg, gw, range(n)), fold, batch)
-    res0h, res0l = split(both_cores(range(n // 2)))
+    def both_cores(which):
+        return jnp.concatenate([take(ref, 0, rp, pw, which) for ref in (sums, sumsq)], axis=0)
+
+    g = unfold_rows(take(sumsq, pw * rp, rg, gw, range(owners)), fold, batch)
+    res0h, res0l = split(both_cores(range(owners // 2)))
     res0f = (jnp.concatenate([res0h] * fold, axis=0), jnp.concatenate([res0l] * fold, axis=0))
-    res1 = both_cores(range(n // 2, n)) - rate * dot3(split(g), res0f)
+    res1 = both_cores(range(owners // 2, owners)) - rate * dot3(split(g), res0f)
     res_s[...] = res1
     for i in range(rows):
         rsend[i : i + 1, :] = res_s[pl.ds((rows + i) * n + place, 1), :]
@@ -238,20 +257,22 @@
     r_copy.wait()
     res_out[:, sib_cols] = rrecv[...]
 
-    def drain(d):
-        p_copy(d).wait_send()
-        q_copy(d).wait_send()
-        a_copy(d).wait_send()
-        b_copy(d).wait_send()
-
-    each(1, n, drain)
+    to_owners(lambda d, at: (p_copy(d, at).wait_send(), q_copy(d, at).wait_send())[0])
+
+    @pl.when(owns(c))
+    def _():
+        each(1, n, lambda d: a_copy(c, d).wait_send())
+        each(1, n, lambda d: b_copy(c, d).wait_send())
+
     each(1, half, lambda e: x_copy(e).wait_send())
     each(0, half, lambda e: f_copy(e).wait_send())
 
 
-def sizes(n, batch, cols):
+def sizes(n, batch, cols, steps):
+    first = n // 4 if n % 8 == 0 else 0
+    owners = n - 2 * first
     fold = max(1, LANES // batch)
-    return fold, batch // fold // n, cols // LANES, pl.cdiv(batch, LANES)
+    return first, owners, fold, steps * batch // 2 // owners, batch // fold // owners, cols // LANES, pl.cdiv(batch, LANES)
 
 
 def fold_rows(g, fold, batch):
@@ -292,8 +313,8 @@
         slot, feats = steps * rows, dataset.shape[1]
         ncen, cols = weights.shape
         total, batch = slot * 2 * n, rows * 2 * n
-        fold, rg, pw, gw = sizes(n, batch, cols)
-        height, extra = pw * slot, gw * rg
+        _, owners, fold, rp, rg, pw, gw = sizes(n, batch, cols, steps)
+        height, extra = pw * rp, gw * rg
         half = n // 2
         vm = pltpu.VMEM
         dma = pltpu.SemaphoreType.DMA
@@ -314,12 +335,12 @@
                 vm((2 * n * slot, ncen), f32),
                 vm((steps, rows, cols), f32),
                 vm((2, total // 2, cols), f32),
+                vm((owners, height, LANES), f32),
                 vm((n, height, LANES), f32),
-                vm((n, height, LANES), f32),
+                vm((owners, height + extra, LANES), f32),
                 vm((n, height + extra, LANES), f32),
-                vm((n, height + extra, LANES), f32),
-                vm((n, height, LANES), f32),
-                vm((n, height + extra, LANES), f32),
+                vm((owners, height, LANES), f32),
+                vm((owners, height + extra, LANES), f32),
                 vm((batch, cols), f32),
                 vm((rows, cols), f32),
                 vm((rows, cols), f32),

time: 27.5 us -> 26.8 us (0.975)
  Pallas kernels: 26 us -> 25.4 us
    pallas_call x1, Pallas kernels: 25.3 us -> 24.7 us  [per_device(): pl.pallas_call(functools.partial(kernel, n), out_shape=outs, in_specs=[an...]
where the time goes in v7:
time: 26.8 us; the launch traced here: 26.7 us
  Pallas kernels  25.4 us (95%)
  between operations  1.29 us (5%)
    pallas_call x1, Pallas kernels, per_device(): pl.pallas_call(functools.partial(kernel, n), out_shape=outs, in_specs=[an...  24.7 us
    pallas_call x1, Pallas kernels, per_device(): pl.pallas_call(hand_over, out_shape=outs, in_specs=[pl.BlockSpec(memory_s...  0.68 us

profile of v7, /device:TPU:0, one launch (start us, length us, event | category | flops | bytes accessed | tf_op | source)
XLA Modules:
  0.0 26.7 jit_solution(1355463974654022776)
XLA Ops:
  1.3 24.7 %shard_map.77 = (f32[128,256]{1,0:T(8,128)S(1)}, f32[4,512]{1,0:T(4,128)S(1)}) custom-call(f32[16,1024]{1,0:T(8,128)} %ds_hbm.1, f32[128,1024]{1,0:T(8,128)} %cen_hbm.1, f32[128,256]{1,0:T(8,128)} %w_hbm.1, s32[2,4]{1,0:T(2,128)} %idx_hbm.1, f32[2,4,512]{2,1,0:T(4,128)} %tgt_hbm.1, f32[1]{0:T(128)S(6)} %copy.8.gam_ref), custom_call_target="tpu_custom_call" | custom-call | tf_op jit(solution)/shard_map/pallas_call | solution.py:326
  26.0 0.7 %shard_map.78 = (f32[128,256]{1,0:T(8,128)}, f32[4,512]{1,0:T(4,128)}) custom-call(f32[128,256]{1,0:T(8,128)S(1)} %get-tuple-element.4.w_in, f32[4,512]{1,0:T(4,128)S(1)} %get-tuple-element.5.res_in), custom_call_target="tpu_custom_call" | custom-call | tf_op jit(solution)/shard_map/pallas_call | solution.py:357
